TPU v7x, 32 devices: a whole 2x2x4 slice. The times are simulated.
32 devices in a mesh: dp: 8 (over z, x), expert: 4 (over y, core).
Axes of the slice: x: 2, y: 2, z: 4, core: 2. Of those that a mesh axis runs over, the one named last changes fastest.
Arguments:
- momentum: float32 [4, 16384, 512], P(None, ('dp', 'expert')), may hold values from -6 to 6
- gradient: bfloat16 [4, 16384, 512], P(None, ('dp', 'expert')), may hold values from -6 to 6
- weights: float32 [4, 16384, 512], P(None, ('dp', 'expert')), may hold values from -0.25 to 0.25
- logit_max: int32 [4, 64], replicated, may hold values from 50 to 799
- clip_flag: int32 [4, 64], replicated, may hold values 0 or 1
Outputs:
- new_weights: float32 [4, 16384, 512], P(None, ('dp', 'expert'))
- new_momentum: float32 [4, 16384, 512], P(None, ('dp', 'expert'))
All inputs are finite; a program needn't handle non-finite values.
Results may differ from a plain program's by a relative error of at most 0.0003.
Values sent between devices are 32-bit elements; how exact they have to be, the bound alone decides.
A program may use at most 128 MiB of HBM per device.

v0:
```python
import math

import jax
import jax.numpy as jnp
from jax import lax
from jax.sharding import PartitionSpec as P

HEADS = 64
NOPE = 128
VDIM = 128
LATENT = 512
ITERS = 3
ROWS = 16384


high = lax.Precision.HIGH
momentum_decay = 0.95
learn_rate = 0.2
weight_decay = 0.1
epsilon = 1e-07
clip_tau = 100.0
coeff_a = 3.4445
coeff_b = -4.775
coeff_c = 2.0315


def product_of(left, right):
    return jnp.matmul(left, right, precision=high, preferred_element_type=jnp.float32)


def chain_of(gram):
    identity = jnp.eye(gram.shape[-1], dtype=jnp.float32)
    product = None
    for step in range(ITERS):
        factor = coeff_a * identity + coeff_b * gram + coeff_c * product_of(gram, gram)
        product = factor if product is None else product_of(product, factor)
        if step + 1 < ITERS:
            gram = product_of(factor, product_of(gram, factor))
    return product


def body(momentum, gradient, weights, logit_max, clip_flag):
    new_momentum = momentum_decay * momentum + gradient.astype(jnp.float32)
    partial = jnp.einsum(
        "mri,mrj->mij", new_momentum, new_momentum, precision=high, preferred_element_type=jnp.float32
    )
    gram = lax.psum_scatter(partial, "expert", scatter_dimension=0, tiled=True)
    gram = lax.psum(gram, "dp")
    squares = jnp.trace(gram, axis1=1, axis2=2)
    inverse = (1.0 / (jnp.sqrt(squares) + epsilon))[:, None, None]
    product = inverse * chain_of(gram * inverse * inverse)
    product = lax.all_gather(product, "expert", axis=0, tiled=True)
    ortho = product_of(new_momentum, product)
    update_scale = 0.2 * math.sqrt(max(ROWS, LATENT))
    stepped = weights - learn_rate * (update_scale * ortho + weight_decay * weights)
    gamma = jnp.where(
        clip_flag == 1, jnp.minimum(1.0, clip_tau / logit_max.astype(jnp.float32)), 1.0
    )
    root = jnp.sqrt(gamma)
    local_rows = weights.shape[1]
    block_index = lax.axis_index("dp") * lax.axis_size("expert") + lax.axis_index("expert")
    row_index = block_index * local_rows + lax.iota(jnp.int32, local_rows)
    head_span = NOPE + VDIM
    head_of = row_index // head_span
    onehot = (head_of[:, None] == lax.iota(jnp.int32, HEADS)[None, :]).astype(jnp.float32)
    row_root = jnp.dot(root, onehot.T, precision=lax.Precision.HIGHEST, preferred_element_type=jnp.float32)
    factor = jnp.where((row_index % head_span < NOPE)[None, :], row_root, 1.0)
    new_weights = stepped * factor[:, :, None]
    return (new_weights, new_momentum)


def solution(mesh):
    return jax.shard_map(
        body,
        mesh=mesh,
        in_specs=(
            P(None, ("dp", "expert"), None),
            P(None, ("dp", "expert"), None),
            P(None, ("dp", "expert"), None),
            P(),
            P(),
        ),
        out_specs=(P(None, ("dp", "expert"), None), P(None, ("dp", "expert"), None)),
        check_vma=False,
    )
```

profile of v0, /device:TPU:0, one launch (start us, length us, event | category | flops | bytes accessed | tf_op | source)
XLA Modules:
  0.0 213.9 jit_solution(17500659330642583936)
XLA Ops:
  7.2 0.0 reduce-scatter.2.cloned.1.call-start
  7.2 3.5 %convert_add_fusion = f32[4,512,512]{2,1,0:T(8,128)S(1)} fusion(bf16[4,512,512]{2,1,0:T(8,128)(2,1)} %param.6, f32[4,512,512]{2,1,0:T(8,128)} %param.5), kind=kLoop, calls=%fused_computation.1 | loop fusion | flops 3145728 | bytes 10485760 | tf_op jit(solution)/shard_map/add | solution.py:43
  10.7 0.0 copy-start
  10.7 2.0 copy-done
  12.7 5.2 %fusion.27 = f32[4,512,512]{2,1,0:T(8,128)} fusion(f32[4,512,512]{2,1,0:T(8,128)S(1)} %convert_add_fusion), kind=kOutput, calls=%fused_computation.48 | convolution fusion | flops 3221225472 | bytes 8388608 | tf_op jit(solution)/shard_map/mri,mrj->mij/dot_general | solution.py:44
  17.9 0.0 reduce-scatter.2.cloned.1.call-update
  18.0 0.0 all-reduce.2.cloned.1.call-start
  18.0 47.3 %reduce-scatter.2.cloned.1.call-done = f32[1,512,512]{2,1,0:T(8,128)} async-done(((f32[4,512,512]{2,1,0:T(8,128)}), f32[1,512,512]{2,1,0:T(8,128)}) %reduce-scatter.2.cloned.1.call-update) | async-done | bytes 1048592 | tf_op jit(solution)/shard_map/reduce_scatter | solution.py:47
  65.3 0.0 all-reduce.2.cloned.1.call-update
  65.4 0.2 all-gather.3.cloned.1.call-start
  65.6 81.7 %all-reduce.2.cloned.1.call-done = f32[1,512,512]{2,1,0:T(8,128)} async-done(((f32[1,512,512]{2,1,0:T(8,128)}), f32[1,512,512]{2,1,0:T(8,128)}) %all-reduce.2.cloned.1.call-update) | async-done | bytes 1048592 | tf_op jit(solution)/shard_map/psum | solution.py:48
  147.3 0.0 copy-start.1
  147.3 2.0 select_reduce_fusion
  150.0 3.3 %fusion.4 = f32[512,512]{1,0:T(8,128)S(1)} fusion(f32[1,512,512]{2,1,0:T(8,128)} %all-reduce.2.cloned.1.call-done, f32[]{:T(128)S(6)} %div.22), kind=kOutput, calls=%fused_computation.12 | convolution fusion | flops 807927808 | bytes 2097156 | tf_op jit(solution)/shard_map/dot_general | solution.py:28
  153.3 0.0 copy-done.1
  153.3 1.0 fusion.5
  154.4 1.0 fusion.28
  155.4 1.1 fusion.1
  156.4 1.0 fusion.30
  157.5 1.0 fusion.29
  158.5 1.0 fusion.31
  159.5 0.0 copy-start.2
  159.5 0.0 copy-start.3
  159.5 1.1 fusion
  160.6 2.0 convolution_multiply_fusion
  162.6 0.0 all-gather.3.cloned.1.call-update
  162.6 0.0 copy-done.2
  162.6 0.0 copy-done.3
  162.6 0.3 convolution_select_fusion
  163.0 33.9 %all-gather.3.cloned.1.call-done = f32[2048,512]{1,0:T(8,128)} async-done(((f32[512,512]{1,0:T(8,128)}), f32[2048,512]{1,0:T(8,128)}) %all-gather.3.cloned.1.call-update) | async-done | bytes 4194320 | tf_op jit(solution)/shard_map/all_gather | solution.py:52
  196.8 10.5 %subtract_multiply_fusion = f32[4,512,512]{2,1,0:T(8,128)} fusion(f32[4,512,512]{2,1,0:T(8,128)} %param.7, f32[4,512,512]{2,1,0:T(8,128)} %copy-done, f32[4,512,512]{2,1,0:T(8,128)} %bitcast.33, f32[4,512]{1,0:T(4,128)S(1)} %convolution_select_fusion), kind=kOutput, calls=%fused_computation | convolution fusion | flops 3227516928 | bytes 16785408 | tf_op jit(solution)/shard_map/dot_general | solution.py:28
  (2 shorter events, 0.0 us)
Async XLA Ops:
  7.2 58.2 %reduce-scatter.2.cloned.1.call-start = ((), (), s32[]{:S(2)}) async-start(), calls=%async_computation.1 | async-start | bytes 5242880 | tf_op jit(solution)/shard_map/reduce_scatter | solution.py:47
  10.7 2.0 copy-start
  18.0 129.3 %all-reduce.2.cloned.1.call-start = ((), (), s32[]{:S(2)}) async-start(), calls=%async_computation.2 | async-start | bytes 2097152 | tf_op jit(solution)/shard_map/psum | solution.py:48
  65.4 131.5 %all-gather.3.cloned.1.call-start = ((), (), s32[]{:S(2)}) async-start(), calls=%async_computation.3 | async-start | bytes 5242880 | tf_op jit(solution)/shard_map/all_gather | solution.py:52
  147.3 6.1 %copy-start.1 = (f32[1,512,512]{2,1,0:T(8,128)S(1)}, f32[1,512,512]{2,1,0:T(8,128)}, u32[]{:S(2)}) copy-start(f32[1,512,512]{2,1,0:T(8,128)} %all-reduce.2.cloned.1.call-done) | copy-start | bytes 3145732
  159.5 3.1 %copy-start.2 = (s32[4,64]{1,0:T(4,128)S(1)}, s32[4,64]{1,0:T(4,128)}, u32[]{:S(2)}) copy-start(s32[4,64]{1,0:T(4,128)} %param.8) | copy-start | bytes 3076
  159.5 3.1 %copy-start.3 = (s32[4,64]{1,0:T(4,128)S(1)}, s32[4,64]{1,0:T(4,128)}, u32[]{:S(2)}) copy-start(s32[4,64]{1,0:T(4,128)} %param.9) | copy-start | bytes 3076
Sparse Core Ops, SparseCore 0:
  18.1 47.2 reduce-scatter.1
  69.2 77.9 all-reduce.1
  162.7 34.0 all-gather.2
where the time goes:
time: 214 us
  waiting for transfers between devices  163 us (76%)
  matrix products  28.5 us (13%)
  between operations  14.6 us (7%)
  other arithmetic  5.5 us (3%)
    psum x1, waiting for transfers between devices, body(): gram = lax.psum(gram, 'dp')  81.7 us
    reduce_scatter x1, waiting for transfers between devices, body(): gram = lax.psum_scatter(partial, 'expert', scatter_dimension=0, tiled=True)  47.3 us
    all_gather x1, waiting for transfers between devices, body(): product = lax.all_gather(product, 'expert', axis=0, tiled=True)  33.9 us
    dot_general x10, matrix products, product_of(): jnp.matmul(left, right, precision=high, preferred_element_type=jnp.float32)  23 us
    dot_general x1, matrix products, body(): jnp.einsum('mri,mrj->mij', new_momentum, new_momentum, precision=high, pr...  5.21 us
  transfers between devices with their start and end apart: 3, of which 3 were waited for; matrix products, arithmetic and copies ran while one was open for 0% of the time, Pallas kernels for 0%

commit v1 on v0

v1 whole, which is shorter than its diff:
```python
import math

import jax
import jax.numpy as jnp
from jax import lax
from jax.experimental import pallas as pl
from jax.experimental.pallas import tpu as pltpu
from jax.sharding import PartitionSpec as P

HEADS = 64
NOPE = 128
VDIM = 128
LATENT = 512
ITERS = 3
ROWS = 16384

momentum_decay = 0.95
learn_rate = 0.2
weight_decay = 0.1
epsilon = 1e-07
clip_tau = 100.0
coeff_a = 3.4445
coeff_b = -4.775
coeff_c = 2.0315

MESH = pl.DeviceIdType.MESH
f32 = jnp.float32
bf16 = jnp.bfloat16
HALF = LATENT // 2
PACK = 3 * HALF
SHARE = PACK // 2
PART = SHARE // 2
CHUNKS = 4
PIECE = SHARE // CHUNKS


def halves(value):
    high = value.astype(bf16)
    return high, (value - high.astype(f32)).astype(bf16)


def dot(left, right):
    return jnp.dot(left, right, preferred_element_type=f32)


def dot_t(left, right):
    return lax.dot_general(left, right, (((1,), (1,)), ((), ())), preferred_element_type=f32)


def dot3(left, right, dot=dot):
    return dot(left[0], right[0]) + (dot(left[0], right[1]) + dot(left[1], right[0]))


def flipped(index, weight):
    bit = (index // weight) % 2
    return index + weight * (1 - 2 * bit), bit


def chain(gsum, ga, gb, q_ref, hi, lo):
    row = lax.broadcasted_iota(jnp.int32, (HALF, HALF), 0)
    col = lax.broadcasted_iota(jnp.int32, (HALF, HALF), 1)
    eye = (row == col).astype(f32)
    g00 = gsum[0:HALF]
    g01 = gsum[HALF : 2 * HALF]
    g11 = gsum[2 * HALF : PACK]
    squares = jnp.sum((g00 + g11) * eye, keepdims=True)
    inverse = 1.0 / (jnp.sqrt(squares) + epsilon)
    inv2 = inverse * inverse

    def put(slot, rows, cols, value):
        high, low = halves(value)
        hi[slot, rows, cols] = high
        lo[slot, rows, cols] = low

    first, second = slice(0, HALF), slice(HALF, LATENT)
    whole = slice(0, LATENT)
    g01 = g01 * inv2
    for rows, cols, value in (
        (first, first, g00 * inv2),
        (first, second, g01),
        (second, first, g01.T),
        (second, second, g11 * inv2),
    ):
        ga[rows, cols] = value
        put(0, rows, cols, value)

    def times(left, right, cols):
        return dot3((hi[left], lo[left]), (hi[right, :, cols], lo[right, :, cols]))

    row = lax.broadcasted_iota(jnp.int32, (LATENT, HALF), 0)
    col = lax.broadcasted_iota(jnp.int32, (LATENT, HALF), 1)
    diagonal = {0: (row == col).astype(f32) * coeff_a, 1: (row == col + HALF).astype(f32) * coeff_a}
    for step in range(ITERS):
        factor_slot = 3 if step == 0 else 1
        for index, cols in enumerate((first, second)):
            factor = diagonal[index] + coeff_b * ga[:, cols] + coeff_c * times(0, 0, cols)
            put(factor_slot, whole, cols, factor)
        if step + 1 < ITERS:
            for cols in (first, second):
                put(2, whole, cols, times(0, factor_slot, cols))
            for cols in (first, second):
                value = times(factor_slot, 2, cols)
                ga[:, cols] = value
                put(0, whole, cols, value)
        if 0 < step < ITERS - 1:
            for cols in (first, second):
                gb[:, cols] = times(3, 1, cols)
            for cols in (first, second):
                put(3, whole, cols, gb[:, cols])
    q_ref[0:HALF] = inverse * dot3((hi[3, first], lo[3, first]), (hi[1, :, first], lo[1, :, first]))
    right = times(3, 1, second)
    q_ref[HALF:PACK] = inverse * right


def exchange_kernel(
    n_dp, n_ex, m_any, g_any, out_a, out_b,
    m_buf, g_buf, gram, from_core, buf_a, buf_b, rec_a, rec_b,
    z_own, z_left, z_right, s_left, s_right, gsum, packed, ga, gb, hi, lo,
    load_sem, core_send, core_recv, plane_send, plane_recv, z_send, z_recv, sum_send, sum_recv,
    back_send, back_recv, last_send, last_recv,
):
    mats = m_buf.shape[0]
    n_y = n_ex // 2
    steps = mats.bit_length() - 1
    d, e = lax.axis_index("dp"), lax.axis_index("expert")
    mate, core = flipped(e, 1)
    other_x, x_bit = flipped(d, 1)
    here, line = d // 2, n_dp // 2
    y = e // 2

    for k in range(mats):
        pltpu.make_async_copy(m_any.at[k], m_buf.at[k], load_sem.at[k, 0]).start()
        pltpu.make_async_copy(g_any.at[k], g_buf.at[k], load_sem.at[k, 1]).start()

    y_bits = []
    weight = n_y // 2
    while weight >= 1:
        partner, bit = flipped(e, 2 * weight)
        y_bits.append(({"expert": partner}, bit))
        weight //= 2
    x_entry = ({"dp": other_x}, x_bit)
    order_a, order_b = [x_entry] + y_bits, y_bits + [x_entry]

    barrier = pltpu.get_barrier_semaphore()
    pl.semaphore_signal(barrier, inc=1, device_id={"expert": mate}, device_id_type=MESH)
    for partner, _ in order_a:
        pl.semaphore_signal(barrier, inc=1, device_id=partner, device_id_type=MESH)

    @pl.when(here > 0)
    def _():
        pl.semaphore_signal(barrier, inc=1, device_id={"dp": d - 2}, device_id_type=MESH)

    @pl.when(here < line - 1)
    def _():
        pl.semaphore_signal(barrier, inc=1, device_id={"dp": d + 2}, device_id_type=MESH)

    ends = (here > 0).astype(jnp.int32) + (here < line - 1).astype(jnp.int32)
    pl.semaphore_wait(barrier, 1 + steps + ends)

    def core_copy(k):
        return pltpu.make_async_remote_copy(
            src_ref=gram.at[k, pl.ds((1 - core) * SHARE, SHARE)],
            dst_ref=from_core.at[k],
            send_sem=core_send.at[k],
            recv_sem=core_recv.at[k],
            device_id={"expert": mate},
            device_id_type=MESH,
        )

    @pl.loop(0, mats)
    def _(k):
        pltpu.make_async_copy(m_any.at[k], m_buf.at[k], load_sem.at[k, 0]).wait()
        pltpu.make_async_copy(g_any.at[k], g_buf.at[k], load_sem.at[k, 1]).wait()
        moved = momentum_decay * m_buf[k] + g_buf[k].astype(f32)
        high, low = halves(moved)
        high_t, low_t = halves(moved.T)
        for at, (i, j) in enumerate(((0, 0), (0, 1), (1, 1))):
            rows, cols = slice(i * HALF, (i + 1) * HALF), slice(j * HALF, (j + 1) * HALF)
            gram[k, at * HALF : (at + 1) * HALF] = dot3(
                (high_t[rows], low_t[rows]), (high[:, cols], low[:, cols])
            )
        core_copy(k).start()

    @pl.loop(0, mats)
    def _(k):
        core_copy(k).wait()
        swapped = (k % n_y) * 2 + k // n_y
        start = pl.multiple_of(core * SHARE, SHARE)
        buf_a[k] = gram[k, pl.ds(start, PART)] + from_core[k, 0:PART]
        buf_b[swapped] = gram[k, pl.ds(start + PART, PART)] + from_core[k, PART:SHARE]

    at_a = at_b = 0
    count, offset = mats, 0
    for step in range(steps):
        count //= 2
        copies = []
        for side, (buf, rec, order, at) in enumerate(
            ((buf_a, rec_a, order_a, at_a), (buf_b, rec_b, order_b, at_b))
        ):
            partner, bit = order[step]
            copy = pltpu.make_async_remote_copy(
                src_ref=buf.at[pl.ds(at + (1 - bit) * count, count)],
                dst_ref=rec.at[pl.ds(offset, count)],
                send_sem=plane_send.at[side, step],
                recv_sem=plane_recv.at[side, step],
                device_id=partner,
                device_id_type=MESH,
            )
            copy.start()
            copies.append(copy)
        at_a = at_a + order_a[step][1] * count
        at_b = at_b + order_b[step][1] * count
        for copy, buf, rec, at in zip(copies, (buf_a, buf_b), (rec_a, rec_b), (at_a, at_b)):
            copy.wait()
            for i in range(count):
                buf[at + i] = buf[at + i] + rec[offset + i]
        offset += count

    per = CHUNKS // 2
    for c in range(CHUNKS):
        source, at = (buf_a, at_a) if c < per else (buf_b, at_b)
        z_own[c] = source[at, (c % per) * PIECE : (c % per + 1) * PIECE]

    @pl.when(here == 0)
    def _():
        z_left[...] = jnp.zeros_like(z_left)

    @pl.when(here == line - 1)
    def _():
        z_right[...] = jnp.zeros_like(z_right)

    def line_copy(way, c):
        source, target = ((s_left, z_left), (s_right, z_right))[way]
        return pltpu.make_async_remote_copy(
            src_ref=source.at[c],
            dst_ref=target.at[c],
            send_sem=z_send.at[way, c],
            recv_sem=z_recv.at[way, c],
            device_id={"dp": d + 2 if way == 0 else d - 2},
            device_id_type=MESH,
        )

    def sum_copy(c):
        rows = pl.ds(pl.multiple_of(core * SHARE + c * PIECE, PIECE), PIECE)
        return pltpu.make_async_remote_copy(
            src_ref=gsum.at[rows],
            dst_ref=gsum.at[rows],
            send_sem=sum_send.at[c],
            recv_sem=sum_recv.at[c],
            device_id={"expert": mate},
            device_id_type=MESH,
        )

    there = line - 1 - here
    far = jnp.maximum(here, there)

    @pl.loop(0, line + CHUNKS - 1)
    def _(t):
        for way, behind in ((0, here), (1, there)):
            source, target = ((s_left, z_left), (s_right, z_right))[way]
            c = t - behind

            @pl.when((c >= 0) & (c < CHUNKS))
            def _():
                @pl.when(behind > 0)
                def _():
                    line_copy(way, c).wait_recv()

                @pl.when(behind < line - 1)
                def _():
                    source[c] = target[c] + z_own[c]
                    line_copy(way, c).start()

        c = t - far

        @pl.when((c >= 0) & (c < CHUNKS))
        def _():
            rows = pl.ds(pl.multiple_of(core * SHARE + c * PIECE, PIECE), PIECE)
            gsum[rows] = (z_left[c] + z_own[c]) + z_right[c]
            sum_copy(c).start()

    @pl.loop(0, CHUNKS)
    def _(c):
        sum_copy(c).wait()

        @pl.when(here < line - 1)
        def _():
            line_copy(0, c).wait_send()

        @pl.when(here > 0)
        def _():
            line_copy(1, c).wait_send()

    chain(gsum, ga, gb, packed, hi, lo)

    own_rows = pl.multiple_of(core * SHARE, SHARE)
    out_a[core, at_a] = packed[pl.ds(own_rows, PART)]
    out_b[core, at_b] = packed[pl.ds(own_rows + PART, PART)]
    count = 1
    pending = []
    news = [(out_a, at_a), (out_b, at_b)]
    starts = [at_a, at_b]
    orders = [order_a, order_b]
    for step in range(steps + 1):
        copies = []
        if step < steps:
            for side, buf in enumerate((out_a, out_b)):
                partner, bit = orders[side][steps - 1 - step]
                block = buf.at[core, pl.ds(starts[side], count)]
                copy = pltpu.make_async_remote_copy(
                    src_ref=block, dst_ref=block,
                    send_sem=back_send.at[side, step], recv_sem=back_recv.at[side, step],
                    device_id=partner, device_id_type=MESH,
                )
                copy.start()
                copies.append(copy)
        fresh = count // 2 if step > 0 else 1
        for side, (buf, at) in enumerate(news):
            block = buf.at[core, pl.ds(at, fresh)]
            copy = pltpu.make_async_remote_copy(
                src_ref=block, dst_ref=block,
                send_sem=last_send.at[side, step], recv_sem=last_recv.at[side, step],
                device_id={"expert": mate}, device_id_type=MESH,
            )
            copy.start()
            pending.append(copy)
        if step < steps:
            news = []
            for side, buf in enumerate((out_a, out_b)):
                copies[side].wait()
                bit = orders[side][steps - 1 - step][1]
                news.append((buf, starts[side] + (1 - 2 * bit) * count))
                starts[side] = starts[side] - bit * count
            count *= 2
    for copy in pending:
        copy.wait()


def exchange(momentum, gradient, n_dp, n_ex):
    mats, rows, width = momentum.shape
    steps = mats.bit_length() - 1
    dma = pltpu.SemaphoreType.DMA
    kernel = lambda *refs: exchange_kernel(n_dp, n_ex, *refs)
    result = jax.ShapeDtypeStruct((2, mats, PART, HALF), f32)
    return pl.pallas_call(
        kernel,
        out_shape=(result, result),
        in_specs=[pl.BlockSpec(memory_space=pl.ANY)] * 2,
        out_specs=[pl.BlockSpec(memory_space=pltpu.VMEM)] * 2,
        scratch_shapes=[
            pltpu.VMEM((mats, rows, width), f32),
            pltpu.VMEM((mats, rows, width), bf16),
            pltpu.VMEM((mats, PACK, HALF), f32),
            pltpu.VMEM((mats, SHARE, HALF), f32),
            pltpu.VMEM((mats, PART, HALF), f32),
            pltpu.VMEM((mats, PART, HALF), f32),
            pltpu.VMEM((mats, PART, HALF), f32),
            pltpu.VMEM((mats, PART, HALF), f32),
        ]
        + [pltpu.VMEM((CHUNKS, PIECE, HALF), f32)] * 5
        + [pltpu.VMEM((PACK, HALF), f32)] * 2
        + [pltpu.VMEM((width, width), f32)] * 2
        + [pltpu.VMEM((4, width, width), bf16)] * 2
        + [dma((mats, 2)), dma((mats,)), dma((mats,))]
        + [dma((2, steps))] * 2
        + [dma((2, CHUNKS))] * 2
        + [dma((CHUNKS,))] * 2
        + [dma((2, steps))] * 2
        + [dma((2, steps + 1))] * 2,
        compiler_params=pltpu.CompilerParams(
            collective_id=0, has_side_effects=True, vmem_limit_bytes=56 * 2**20
        ),
        name="exchange",
    )(momentum, gradient)


def update_kernel(
    span, local_rows, n_ex, logit_ref, flag_ref, m_ref, g_ref, w_ref, a_ref, b_ref, w_out, m_out,
):
    k, tile = pl.program_id(0), pl.program_id(1)
    rows = m_ref.shape[1]
    moved = momentum_decay * m_ref[0] + g_ref[0].astype(f32)
    m_out[0] = moved
    high, low = halves(moved)
    pack = jnp.concatenate([a_ref[0, 0], b_ref[0, 0], a_ref[1, 0], b_ref[1, 0]], axis=0)
    pack_hi, pack_lo = halves(pack)
    p00, p01, p11 = [
        (pack_hi[i * HALF : (i + 1) * HALF], pack_lo[i * HALF : (i + 1) * HALF]) for i in range(3)
    ]
    x0 = (high[:, :HALF], low[:, :HALF])
    x1 = (high[:, HALF:], low[:, HALF:])
    ortho = (dot3(x0, p00) + dot3(x1, p01, dot_t), dot3(x0, p01) + dot3(x1, p11))
    update_scale = 0.2 * math.sqrt(max(ROWS, LATENT))
    first = (lax.axis_index("dp") * n_ex + lax.axis_index("expert")) * local_rows + tile * rows
    for i in range(rows // span):
        row = first + i * span
        head = row // (NOPE + VDIM)
        logit = jnp.full((1, HALF), logit_ref[k, head], jnp.int32).astype(f32)
        use = jnp.full((1, HALF), flag_ref[k, head], jnp.int32) == 1
        keyed = jnp.full((1, HALF), row % (NOPE + VDIM), jnp.int32) < NOPE
        root = jnp.sqrt(jnp.minimum(1.0, clip_tau / logit))
        factor = jnp.where(use & keyed, root, 1.0)
        at = slice(i * span, (i + 1) * span)
        for j in range(2):
            cols = slice(j * HALF, (j + 1) * HALF)
            weight = w_ref[0, at, cols]
            stepped = weight - learn_rate * (
                update_scale * ortho[j][at] + weight_decay * weight
            )
            w_out[0, at, cols] = stepped * factor


def update(momentum, gradient, weights, logit_max, clip_flag, part_a, part_b, n_ex):
    mats, local_rows, width = momentum.shape
    rows = min(local_rows, 256)
    span = min(rows, NOPE)
    n_y = n_ex // 2
    block = pl.BlockSpec((1, rows, width), lambda k, i: (k, i, 0))
    scalar = pl.BlockSpec(memory_space=pltpu.SMEM)
    result = jax.ShapeDtypeStruct(momentum.shape, f32)
    kernel = lambda *refs: update_kernel(span, local_rows, n_ex, *refs)
    return pl.pallas_call(
        kernel,
        grid=(mats, local_rows // rows),
        out_shape=(result, result),
        in_specs=[
            scalar, scalar, block, block, block,
            pl.BlockSpec((2, 1, PART, HALF), lambda k, i: (0, k, 0, 0)),
            pl.BlockSpec((2, 1, PART, HALF), lambda k, i: (0, (k % n_y) * 2 + k // n_y, 0, 0)),
        ],
        out_specs=[block, block],
        compiler_params=pltpu.CompilerParams(vmem_limit_bytes=40 * 2**20),
        name="update",
    )(logit_max, clip_flag, momentum, gradient, weights, part_a, part_b)


def solution(mesh):
    n_dp, n_ex = mesh.shape["dp"], mesh.shape["expert"]

    def body(momentum, gradient, weights, logit_max, clip_flag):
        part_a, part_b = exchange(momentum, gradient, n_dp, n_ex)
        return update(
            momentum, gradient, weights, logit_max, clip_flag, part_a, part_b, n_ex
        )

    spec = P(None, ("dp", "expert"), None)
    return jax.shard_map(
        body,
        mesh=mesh,
        in_specs=(spec, spec, spec, P(), P()),
        out_specs=(spec, spec),
        check_vma=False,
    )
```

time: 214 us -> 92.7 us (0.43)
  waiting for transfers between devices: 163 us -> 0 us
  Pallas kernels: 0 us -> 86 us
  matrix products: 28.5 us -> 0 us
  between operations: 14.6 us -> 0.7 us
  other arithmetic: 5.5 us -> 0 us
  local copies, waits for them, and re-layouts: 2.02 us -> 5.69 us
    pallas_call x0 -> x2, Pallas kernels: none -> 86 us  [the longest x1 78.8 us: exchange(): pl.pallas_call(kernel, out_shape=(result, result), in_specs=[pl.BlockSpec...]
    psum x1 -> x0, waiting for transfers between devices: 81.7 us -> none  [body(): gram = lax.psum(gram, 'dp')]
    reduce_scatter x1 -> x0, waiting for transfers between devices: 47.3 us -> none  [body(): gram = lax.psum_scatter(partial, 'expert', scatter_dimension=0, tiled=True)]
    all_gather x1 -> x0, waiting for transfers between devices: 33.9 us -> none  [body(): product = lax.all_gather(product, 'expert', axis=0, tiled=True)]
    dot_general x12 -> x0, matrix products: 28.5 us -> none  [the longest x10 23 us: product_of(): jnp.matmul(left, right, precision=high, preferred_element_type=jnp.float32)]
    unnamed x8 -> x14, local copies, waits for them, and re-layouts: 2.02 us -> 5.69 us
    add x1 -> x0, other arithmetic: 3.49 us -> none  [body(): new_momentum = momentum_decay * momentum + gradient.astype(jnp.float32)]
  transfers between devices with their start and end apart: 3 -> 0, of which waited for: 3 -> 0; matrix products, arithmetic and copies ran while one was open for 0% -> 0% of each run, Pallas kernels for 0% -> 0%
where the time goes in v1:
time: 92.7 us; the launch traced here: 92.4 us
  Pallas kernels  86 us (93%)
  local copies, waits for them, and re-layouts  5.69 us (6%)
    pallas_call x1, Pallas kernels, exchange(): pl.pallas_call(kernel, out_shape=(result, result), in_specs=[pl.BlockSpec...  78.8 us
    pallas_call x1, Pallas kernels, update(): pl.pallas_call(kernel, grid=(mats, local_rows // rows), out_shape=(result...  7.28 us
    unnamed x14, local copies, waits for them, and re-layouts  5.69 us

profile of v1, /device:TPU:0, one launch (start us, length us, event | category | flops | bytes accessed | tf_op | source)
XLA Modules:
  0.0 92.4 jit_solution(8526402254075127460)
XLA Ops:
  0.6 0.0 copy-start.1
  0.6 0.0 copy-start
  0.6 0.0 copy-start.5
  0.7 78.8 %exchange.1 = (f32[2,4,192,256]{3,2,1,0:T(8,128)}, f32[2,4,192,256]{3,2,1,0:T(8,128)}) custom-call(f32[4,512,512]{2,1,0:T(8,128)} %refs_2_.1, bf16[4,512,512]{2,1,0:T(8,128)(2,1)} %refs_3_.1), custom_call_target="tpu_custom_call" | custom-call | tf_op jit(solution)/shard_map/exchange/pallas_call | solution.py:345
  79.4 0.0 copy-done.1
  79.4 0.0 copy-done
  79.4 0.0 copy-done.5
  79.4 0.0 copy-start.2
  79.5 2.2 %copy-done.2 = f32[4,512,512]{2,1,0:T(8,128)S(1)} copy-done((f32[4,512,512]{2,1,0:T(8,128)S(1)}, f32[4,512,512]{2,1,0:T(8,128)}, u32[]{:S(2)}) %copy-start.2) | copy-done | bytes 4194328
  81.6 0.0 copy-start.3
  81.6 1.4 %copy-done.3 = f32[2,4,192,256]{3,2,1,0:T(8,128)S(1)} copy-done((f32[2,4,192,256]{3,2,1,0:T(8,128)S(1)}, f32[2,4,192,256]{3,2,1,0:T(8,128)}, u32[]{:S(2)}) %copy-start.3) | copy-done | bytes 1572888
  83.0 0.0 copy-start.4
  83.1 1.4 %copy-done.4 = f32[2,4,192,256]{3,2,1,0:T(8,128)S(1)} copy-done((f32[2,4,192,256]{3,2,1,0:T(8,128)S(1)}, f32[2,4,192,256]{3,2,1,0:T(8,128)}, u32[]{:S(2)}) %copy-start.4) | copy-done | bytes 1572888
  84.5 0.0 copy-start.6
  84.5 0.7 copy-done.6
  85.1 7.3 %update.1 = (f32[4,512,512]{2,1,0:T(8,128)}, f32[4,512,512]{2,1,0:T(8,128)}) custom-call(s32[4,64]{1,0:T(4,128)S(1)} %copy-done.5, s32[4,64]{1,0:T(4,128)S(1)} %copy-done.6, f32[4,512,512]{2,1,0:T(8,128)S(1)} %copy-done, bf16[4,512,512]{2,1,0:T(8,128)(2,1)S(1)} %copy-done.1, f32[4,512,512]{2,1,0:T(8,128)S(1)} %copy-done.2, f32[2,4,192,256]{3,2,1,0:T(8,128)S(1)} %copy-done.3, ...), custom_call_target="tpu_custom_call" | custom-call | tf_op jit(solution)/shard_map/update/pallas_call | solution.py:422
Async XLA Ops:
  0.6 78.8 %copy-start.1 = (bf16[4,512,512]{2,1,0:T(8,128)(2,1)S(1)}, bf16[4,512,512]{2,1,0:T(8,128)(2,1)}, u32[]{:S(2)}) copy-start(bf16[4,512,512]{2,1,0:T(8,128)(2,1)} %refs_3_.1) | copy-start | bytes 6291460
  0.6 78.8 %copy-start = (f32[4,512,512]{2,1,0:T(8,128)S(1)}, f32[4,512,512]{2,1,0:T(8,128)}, u32[]{:S(2)}) copy-start(f32[4,512,512]{2,1,0:T(8,128)} %refs_2_.1) | copy-start | bytes 12582916
  0.6 78.8 %copy-start.5 = (s32[4,64]{1,0:T(4,128)S(1)}, s32[4,64]{1,0:T(4,128)}, u32[]{:S(2)}) copy-start(s32[4,64]{1,0:T(4,128)} %refs_0_.3) | copy-start | bytes 3076
  79.4 2.2 %copy-start.2 = (f32[4,512,512]{2,1,0:T(8,128)S(1)}, f32[4,512,512]{2,1,0:T(8,128)}, u32[]{:S(2)}) copy-start(f32[4,512,512]{2,1,0:T(8,128)} %refs_4_.1) | copy-start | bytes 12582916
  81.6 1.4 %copy-start.3 = (f32[2,4,192,256]{3,2,1,0:T(8,128)S(1)}, f32[2,4,192,256]{3,2,1,0:T(8,128)}, u32[]{:S(2)}) copy-start(f32[2,4,192,256]{3,2,1,0:T(8,128)} %get-tuple-element.4.refs_5_) | copy-start | bytes 4718596
  83.0 1.4 %copy-start.4 = (f32[2,4,192,256]{3,2,1,0:T(8,128)S(1)}, f32[2,4,192,256]{3,2,1,0:T(8,128)}, u32[]{:S(2)}) copy-start(f32[2,4,192,256]{3,2,1,0:T(8,128)} %get-tuple-element.5.refs_6_) | copy-start | bytes 4718596
  84.5 0.7 copy-start.6

commit v2 on v1

--- a/solution.py
+++ b/solution.py
@@ -30,7 +30,7 @@
 PACK = 3 * HALF
 SHARE = PACK // 2
 PART = SHARE // 2
-CHUNKS = 4
+CHUNKS = 8
 PIECE = SHARE // CHUNKS
 
 
@@ -114,10 +114,10 @@
 
 def exchange_kernel(
     n_dp, n_ex, m_any, g_any, out_a, out_b,
-    m_buf, g_buf, gram, from_core, buf_a, buf_b, rec_a, rec_b,
+    m_buf, g_buf, gram, from_core, buf, rec,
     z_own, z_left, z_right, s_left, s_right, gsum, packed, ga, gb, hi, lo,
     load_sem, core_send, core_recv, plane_send, plane_recv, z_send, z_recv, sum_send, sum_recv,
-    back_send, back_recv, last_send, last_recv,
+    back_send, back_recv,
 ):
     mats = m_buf.shape[0]
     n_y = n_ex // 2
@@ -186,40 +186,82 @@
         core_copy(k).wait()
         swapped = (k % n_y) * 2 + k // n_y
         start = pl.multiple_of(core * SHARE, SHARE)
-        buf_a[k] = gram[k, pl.ds(start, PART)] + from_core[k, 0:PART]
-        buf_b[swapped] = gram[k, pl.ds(start + PART, PART)] + from_core[k, PART:SHARE]
-
-    at_a = at_b = 0
-    count, offset = mats, 0
-    for step in range(steps):
-        count //= 2
-        copies = []
-        for side, (buf, rec, order, at) in enumerate(
-            ((buf_a, rec_a, order_a, at_a), (buf_b, rec_b, order_b, at_b))
-        ):
-            partner, bit = order[step]
-            copy = pltpu.make_async_remote_copy(
-                src_ref=buf.at[pl.ds(at + (1 - bit) * count, count)],
-                dst_ref=rec.at[pl.ds(offset, count)],
-                send_sem=plane_send.at[side, step],
-                recv_sem=plane_recv.at[side, step],
+        for c in range(CHUNKS):
+            own = gram[k, pl.ds(start + c * PIECE, PIECE)]
+            buf[c, k if c % 2 == 0 else swapped] = own + from_core[k, c * PIECE : (c + 1) * PIECE]
+
+    def pick(side, first, second):
+        return first + side * (second - first)
+
+    def target_of(partner):
+        return partner.get("dp", d), partner.get("expert", e)
+
+    def route(c, step):
+        side = c % 2
+        at, count = 0, mats
+        for i in range(step + 1):
+            bit = pick(side, order_a[i][1], order_b[i][1])
+            if i < step:
+                count //= 2
+                at = at + bit * count
+        first, second = target_of(order_a[step][0]), target_of(order_b[step][0])
+        partner = (pick(side, first[0], second[0]), pick(side, first[1], second[1]))
+        return at, count // 2, bit, partner
+
+    def plane_copies(c, step):
+        at, count, bit, partner = route(c, step)
+        offset = mats - 2 * count
+        source = at + (1 - bit) * count
+        if step + 1 < steps:
+            half = count // 2
+            next_bit = pick(c % 2, order_a[step + 1][1], order_b[step + 1][1])
+            spans = [(0, (1 - next_bit) * half, half), (1, next_bit * half, half)]
+        else:
+            spans = [(0, 0, count)]
+        return [
+            pltpu.make_async_remote_copy(
+                src_ref=buf.at[c, pl.ds(source + shift, size)],
+                dst_ref=rec.at[c, pl.ds(offset + shift, size)],
+                send_sem=plane_send.at[step, i, c],
+                recv_sem=plane_recv.at[step, i, c],
                 device_id=partner,
                 device_id_type=MESH,
             )
+            for i, shift, size in spans
+        ]
+
+    def take(c, step):
+        at, count, bit, _ = route(c, step)
+        offset = mats - 2 * count
+        keep = at + bit * count
+        copies = plane_copies(c, step)
+        if step + 1 < steps:
+            half = count // 2
+            next_bit = pick(c % 2, order_a[step + 1][1], order_b[step + 1][1])
+            shifts = [(1 - next_bit) * half, next_bit * half]
+        else:
+            half, shifts = count, [0]
+        for i, shift in enumerate(shifts):
+            copies[i].wait_recv()
+            for j in range(half):
+                total = buf[c, keep + shift + j] + rec[c, offset + shift + j]
+                if step + 1 < steps:
+                    buf[c, keep + shift + j] = total
+                else:
+                    z_own[c] = total
+            if i == 0 and step + 1 < steps:
+                for copy in plane_copies(c, step + 1):
+                    copy.start()
+
+    @pl.loop(0, CHUNKS)
+    def _(c):
+        for copy in plane_copies(c, 0):
             copy.start()
-            copies.append(copy)
-        at_a = at_a + order_a[step][1] * count
-        at_b = at_b + order_b[step][1] * count
-        for copy, buf, rec, at in zip(copies, (buf_a, buf_b), (rec_a, rec_b), (at_a, at_b)):
-            copy.wait()
-            for i in range(count):
-                buf[at + i] = buf[at + i] + rec[offset + i]
-        offset += count
-
-    per = CHUNKS // 2
-    for c in range(CHUNKS):
-        source, at = (buf_a, at_a) if c < per else (buf_b, at_b)
-        z_own[c] = source[at, (c % per) * PIECE : (c % per + 1) * PIECE]
+
+    at_a = at_b = 0
+    for step in range(steps):
+        at_a = at_a + order_a[step][1] * (mats >> (step + 1))
+        at_b = at_b + order_b[step][1] * (mats >> (step + 1))
 
     @pl.when(here == 0)
     def _():
@@ -254,8 +296,17 @@
     there = line - 1 - here
     far = jnp.maximum(here, there)
 
-    @pl.loop(0, line + CHUNKS - 1)
-    def _(t):
+    lag = steps - 1
+
+    @pl.loop(0, line + CHUNKS - 1 + lag)
+    def _(u):
+        for step in range(steps):
+
+            @pl.when((u >= step) & (u - step < CHUNKS))
+            def _():
+                take(u - step, step)
+
+        t = u - lag
         for way, behind in ((0, here), (1, there)):
             source, target = ((s_left, z_left), (s_right, z_right))[way]
             c = t - behind
@@ -282,6 +333,9 @@
     @pl.loop(0, CHUNKS)
     def _(c):
         sum_copy(c).wait()
+        for step in range(steps):
+            for copy in plane_copies(c, step):
+                copy.wait_send()
 
         @pl.when(here < line - 1)
         def _():
@@ -293,47 +347,45 @@
 
     chain(gsum, ga, gb, packed, hi, lo)
 
-    own_rows = pl.multiple_of(core * SHARE, SHARE)
-    out_a[core, at_a] = packed[pl.ds(own_rows, PART)]
-    out_b[core, at_b] = packed[pl.ds(own_rows + PART, PART)]
-    count = 1
-    pending = []
-    news = [(out_a, at_a), (out_b, at_b)]
-    starts = [at_a, at_b]
-    orders = [order_a, order_b]
+    sides = []
+    for buf_out, at, order, odd in ((out_a, at_a, order_a, 0), (out_b, at_b, order_b, 1)):
+        for q in range(CHUNKS // 2):
+            rows = pl.multiple_of(core * SHARE + (2 * q + odd) * PIECE, PIECE)
+            buf_out[core, at, q * PIECE : (q + 1) * PIECE] = packed[pl.ds(rows, PIECE)]
+        back = order[::-1]
+        sides.append((buf_out, at, back, odd))
+
+    def back_copy(side, step, block):
+        buf_out, at, back, odd = sides[side]
+        slot = at
+        for i in range(steps):
+            if (block >> i) % 2:
+                slot = slot + (1 - 2 * back[i][1]) * (1 << i)
+        ref = buf_out.at[core, slot]
+        return pltpu.make_async_remote_copy(
+            src_ref=ref,
+            dst_ref=ref,
+            send_sem=back_send.at[side, (1 << step) - 1 + block],
+            recv_sem=back_recv.at[side, (1 << step) - 1 + block],
+            device_id=back[step][0] if step < steps else {"expert": mate},
+            device_id_type=MESH,
+        )
+
+    for block in range(mats):
+        for side in range(2):
+            if block > 0:
+                top = block.bit_length() - 1
+                back_copy(side, top, block - (1 << top)).wait_recv()
+            for step in range(steps, -1, -1):
+                if (1 << step) > block:
+                    back_copy(side, step, block).start()
+    for block in range(mats):
+        for side in range(2):
+            back_copy(side, steps, block).wait_recv()
     for step in range(steps + 1):
-        copies = []
-        if step < steps:
-            for side, buf in enumerate((out_a, out_b)):
-                partner, bit = orders[side][steps - 1 - step]
-                block = buf.at[core, pl.ds(starts[side], count)]
-                copy = pltpu.make_async_remote_copy(
-                    src_ref=block, dst_ref=block,
-                    send_sem=back_send.at[side, step], recv_sem=back_recv.at[side, step],
-                    device_id=partner, device_id_type=MESH,
-                )
-                copy.start()
-                copies.append(copy)
-        fresh = count // 2 if step > 0 else 1
-        for side, (buf, at) in enumerate(news):
-            block = buf.at[core, pl.ds(at, fresh)]
-            copy = pltpu.make_async_remote_copy(
-                src_ref=block, dst_ref=block,
-                send_sem=last_send.at[side, step], recv_sem=last_recv.at[side, step],
-                device_id={"expert": mate}, device_id_type=MESH,
-            )
-            copy.start()
-            pending.append(copy)
-        if step < steps:
-            news = []
-            for side, buf in enumerate((out_a, out_b)):
-                copies[side].wait()
-                bit = orders[side][steps - 1 - step][1]
-                news.append((buf, starts[side] + (1 - 2 * bit) * count))
-                starts[side] = starts[side] - bit * count
-            count *= 2
-    for copy in pending:
-        copy.wait()
+        for block in range(1 << step):
+            for side in range(2):
+                back_copy(side, step, block).wait_send()
 
 
 def exchange(momentum, gradient, n_dp, n_ex):
@@ -352,23 +404,20 @@
             pltpu.VMEM((mats, rows, width), bf16),
             pltpu.VMEM((mats, PACK, HALF), f32),
             pltpu.VMEM((mats, SHARE, HALF), f32),
-            pltpu.VMEM((mats, PART, HALF), f32),
-            pltpu.VMEM((mats, PART, HALF), f32),
-            pltpu.VMEM((mats, PART, HALF), f32),
-            pltpu.VMEM((mats, PART, HALF), f32),
+            pltpu.VMEM((CHUNKS, mats, PIECE, HALF), f32),
+            pltpu.VMEM((CHUNKS, mats, PIECE, HALF), f32),
         ]
         + [pltpu.VMEM((CHUNKS, PIECE, HALF), f32)] * 5
         + [pltpu.VMEM((PACK, HALF), f32)] * 2
         + [pltpu.VMEM((width, width), f32)] * 2
         + [pltpu.VMEM((4, width, width), bf16)] * 2
         + [dma((mats, 2)), dma((mats,)), dma((mats,))]
-        + [dma((2, steps))] * 2
+        + [dma((steps, 2, CHUNKS))] * 2
         + [dma((2, CHUNKS))] * 2
         + [dma((CHUNKS,))] * 2
-        + [dma((2, steps))] * 2
-        + [dma((2, steps + 1))] * 2,
+        + [dma((2, 2 * mats - 1))] * 2,
         compiler_params=pltpu.CompilerParams(
-            collective_id=0, has_side_effects=True, vmem_limit_bytes=56 * 2**20
+            collective_id=0, has_side_effects=True, vmem_limit_bytes=32 * 2**20
         ),
         name="exchange",
     )(momentum, gradient)
@@ -382,7 +431,15 @@
     moved = momentum_decay * m_ref[0] + g_ref[0].astype(f32)
     m_out[0] = moved
     high, low = halves(moved)
-    pack = jnp.concatenate([a_ref[0, 0], b_ref[0, 0], a_ref[1, 0], b_ref[1, 0]], axis=0)
+    pack = jnp.concatenate(
+        [
+            ref[core, 0, q * PIECE : (q + 1) * PIECE]
+            for core in range(2)
+            for q in range(CHUNKS // 2)
+            for ref in (a_ref, b_ref)
+        ],
+        axis=0,
+    )
     pack_hi, pack_lo = halves(pack)
     p00, p01, p11 = [
         (pack_hi[i * HALF : (i + 1) * HALF], pack_lo[i * HALF : (i + 1) * HALF]) for i in range(3)
@@ -429,7 +486,7 @@
             pl.BlockSpec((2, 1, PART, HALF), lambda k, i: (0, (k % n_y) * 2 + k // n_y, 0, 0)),
         ],
         out_specs=[block, block],
-        compiler_params=pltpu.CompilerParams(vmem_limit_bytes=40 * 2**20),
+        compiler_params=pltpu.CompilerParams(vmem_limit_bytes=20 * 2**20),
         name="update",
     )(logit_max, clip_flag, momentum, gradient, weights, part_a, part_b)
 

time: 92.7 us -> 93.7 us (1.011)
    unnamed x14 -> x12, local copies, waits for them, and re-layouts: 5.69 us -> 5.97 us
where the time goes in v2:
time: 93.7 us; the launch traced here: 93.5 us
  Pallas kernels  86.9 us (93%)
  local copies, waits for them, and re-layouts  5.97 us (6%)
    pallas_call x1, Pallas kernels, exchange(): pl.pallas_call(kernel, out_shape=(result, result), in_specs=[pl.BlockSpec...  79.6 us
    pallas_call x1, Pallas kernels, update(): pl.pallas_call(kernel, grid=(mats, local_rows // rows), out_shape=(result...  7.28 us
    unnamed x12, local copies, waits for them, and re-layouts  5.97 us

profile of v2, /device:TPU:0, one launch (start us, length us, event | category | flops | bytes accessed | tf_op | source)
XLA Modules:
  0.0 93.5 jit_solution(2356336055317037840)
XLA Ops:
  0.6 0.0 copy-start
  0.6 2.2 %copy-done = f32[4,512,512]{2,1,0:T(8,128)S(1)} copy-done((f32[4,512,512]{2,1,0:T(8,128)S(1)}, f32[4,512,512]{2,1,0:T(8,128)}, u32[]{:S(2)}) %copy-start) | copy-done | bytes 4194328
  2.8 0.0 copy-start.2
  2.8 1.6 %copy-done.2 = bf16[4,512,512]{2,1,0:T(8,128)(2,1)S(1)} copy-done((bf16[4,512,512]{2,1,0:T(8,128)(2,1)S(1)}, bf16[4,512,512]{2,1,0:T(8,128)(2,1)}, u32[]{:S(2)}) %copy-start.2) | copy-done | bytes 2097176
  4.4 0.0 copy-start.1
  4.4 0.0 copy-start.4
  4.4 0.0 copy-start.5
  4.4 79.6 %exchange.1 = (f32[2,4,192,256]{3,2,1,0:T(8,128)S(1)}, f32[2,4,192,256]{3,2,1,0:T(8,128)S(1)}) custom-call(f32[4,512,512]{2,1,0:T(8,128)S(1)} %copy-done, bf16[4,512,512]{2,1,0:T(8,128)(2,1)S(1)} %copy-done.2), custom_call_target="tpu_custom_call" | custom-call | tf_op jit(solution)/shard_map/exchange/pallas_call | solution.py:397
  84.0 0.0 copy-done.1
  84.0 0.0 copy-done.4
  84.0 0.0 copy-done.5
  84.0 0.0 copy-start.3
  84.1 2.2 %copy-done.3 = f32[4,512,512]{2,1,0:T(8,128)S(1)} copy-done((f32[4,512,512]{2,1,0:T(8,128)S(1)}, f32[4,512,512]{2,1,0:T(8,128)}, u32[]{:S(2)}) %copy-start.3) | copy-done | bytes 4194328
  86.2 7.3 %update.1 = (f32[4,512,512]{2,1,0:T(8,128)}, f32[4,512,512]{2,1,0:T(8,128)}) custom-call(s32[4,64]{1,0:T(4,128)S(1)} %copy-done.4, s32[4,64]{1,0:T(4,128)S(1)} %copy-done.5, f32[4,512,512]{2,1,0:T(8,128)S(1)} %copy-done.1, bf16[4,512,512]{2,1,0:T(8,128)(2,1)S(1)} %copy-done.2, f32[4,512,512]{2,1,0:T(8,128)S(1)} %copy-done.3, ...), custom_call_target="tpu_custom_call" | custom-call | tf_op jit(solution)/shard_map/update/pallas_call | solution.py:479
Async XLA Ops:
  0.6 2.2 %copy-start = (f32[4,512,512]{2,1,0:T(8,128)S(1)}, f32[4,512,512]{2,1,0:T(8,128)}, u32[]{:S(2)}) copy-start(f32[4,512,512]{2,1,0:T(8,128)} %refs_2_.1) | copy-start | bytes 12582916
  2.8 1.6 %copy-start.2 = (bf16[4,512,512]{2,1,0:T(8,128)(2,1)S(1)}, bf16[4,512,512]{2,1,0:T(8,128)(2,1)}, u32[]{:S(2)}) copy-start(bf16[4,512,512]{2,1,0:T(8,128)(2,1)} %refs_3_.1) | copy-start | bytes 6291460
  4.4 79.6 %copy-start.1 = (f32[4,512,512]{2,1,0:T(8,128)S(1)}, f32[4,512,512]{2,1,0:T(8,128)}, u32[]{:S(2)}) copy-start(f32[4,512,512]{2,1,0:T(8,128)} %refs_2_.1) | copy-start | bytes 12582916
  4.4 79.6 %copy-start.4 = (s32[4,64]{1,0:T(4,128)S(1)}, s32[4,64]{1,0:T(4,128)}, u32[]{:S(2)}) copy-start(s32[4,64]{1,0:T(4,128)} %refs_0_.3) | copy-start | bytes 3076
  4.4 79.6 %copy-start.5 = (s32[4,64]{1,0:T(4,128)S(1)}, s32[4,64]{1,0:T(4,128)}, u32[]{:S(2)}) copy-start(s32[4,64]{1,0:T(4,128)} %refs_1_.3) | copy-start | bytes 3076
  84.0 2.2 %copy-start.3 = (f32[4,512,512]{2,1,0:T(8,128)S(1)}, f32[4,512,512]{2,1,0:T(8,128)}, u32[]{:S(2)}) copy-start(f32[4,512,512]{2,1,0:T(8,128)} %refs_4_.1) | copy-start | bytes 12582916

commit v3 on v2

--- a/solution.py
+++ b/solution.py
@@ -30,7 +30,7 @@
 PACK = 3 * HALF
 SHARE = PACK // 2
 PART = SHARE // 2
-CHUNKS = 8
+CHUNKS = 4
 PIECE = SHARE // CHUNKS
 
 

time: 93.7 us -> 87.6 us (0.935)
  Pallas kernels: 86.9 us -> 80.8 us
    pallas_call x1, Pallas kernels: 79.6 us -> 73.5 us  [exchange(): pl.pallas_call(kernel, out_shape=(result, result), in_specs=[pl.BlockSpec...]
where the time goes in v3:
time: 87.6 us; the launch traced here: 87.4 us
  Pallas kernels  80.8 us (92%)
  local copies, waits for them, and re-layouts  5.97 us (7%)
    pallas_call x1, Pallas kernels, exchange(): pl.pallas_call(kernel, out_shape=(result, result), in_specs=[pl.BlockSpec...  73.5 us
    pallas_call x1, Pallas kernels, update(): pl.pallas_call(kernel, grid=(mats, local_rows // rows), out_shape=(result...  7.29 us
    unnamed x12, local copies, waits for them, and re-layouts  5.97 us

profile of v3, /device:TPU:0, one launch (start us, length us, event | category | flops | bytes accessed | tf_op | source)
XLA Modules:
  0.0 87.4 jit_solution(17413581878634131365)
XLA Ops:
  0.6 0.0 copy-start
  0.6 2.2 %copy-done = f32[4,512,512]{2,1,0:T(8,128)S(1)} copy-done((f32[4,512,512]{2,1,0:T(8,128)S(1)}, f32[4,512,512]{2,1,0:T(8,128)}, u32[]{:S(2)}) %copy-start) | copy-done | bytes 4194328
  2.8 0.0 copy-start.2
  2.8 1.6 %copy-done.2 = bf16[4,512,512]{2,1,0:T(8,128)(2,1)S(1)} copy-done((bf16[4,512,512]{2,1,0:T(8,128)(2,1)S(1)}, bf16[4,512,512]{2,1,0:T(8,128)(2,1)}, u32[]{:S(2)}) %copy-start.2) | copy-done | bytes 2097176
  4.4 0.0 copy-start.1
  4.4 0.0 copy-start.4
  4.4 0.0 copy-start.5
  4.4 73.5 %exchange.1 = (f32[2,4,192,256]{3,2,1,0:T(8,128)S(1)}, f32[2,4,192,256]{3,2,1,0:T(8,128)S(1)}) custom-call(f32[4,512,512]{2,1,0:T(8,128)S(1)} %copy-done, bf16[4,512,512]{2,1,0:T(8,128)(2,1)S(1)} %copy-done.2), custom_call_target="tpu_custom_call" | custom-call | tf_op jit(solution)/shard_map/exchange/pallas_call | solution.py:397
  77.9 0.0 copy-done.1
  77.9 0.0 copy-done.4
  77.9 0.0 copy-done.5
  77.9 0.0 copy-start.3
  77.9 2.2 %copy-done.3 = f32[4,512,512]{2,1,0:T(8,128)S(1)} copy-done((f32[4,512,512]{2,1,0:T(8,128)S(1)}, f32[4,512,512]{2,1,0:T(8,128)}, u32[]{:S(2)}) %copy-start.3) | copy-done | bytes 4194328
  80.1 7.3 %update.1 = (f32[4,512,512]{2,1,0:T(8,128)}, f32[4,512,512]{2,1,0:T(8,128)}) custom-call(s32[4,64]{1,0:T(4,128)S(1)} %copy-done.4, s32[4,64]{1,0:T(4,128)S(1)} %copy-done.5, f32[4,512,512]{2,1,0:T(8,128)S(1)} %copy-done.1, bf16[4,512,512]{2,1,0:T(8,128)(2,1)S(1)} %copy-done.2, f32[4,512,512]{2,1,0:T(8,128)S(1)} %copy-done.3, ...), custom_call_target="tpu_custom_call" | custom-call | tf_op jit(solution)/shard_map/update/pallas_call | solution.py:479
Async XLA Ops:
  0.6 2.2 %copy-start = (f32[4,512,512]{2,1,0:T(8,128)S(1)}, f32[4,512,512]{2,1,0:T(8,128)}, u32[]{:S(2)}) copy-start(f32[4,512,512]{2,1,0:T(8,128)} %refs_2_.1) | copy-start | bytes 12582916
  2.8 1.6 %copy-start.2 = (bf16[4,512,512]{2,1,0:T(8,128)(2,1)S(1)}, bf16[4,512,512]{2,1,0:T(8,128)(2,1)}, u32[]{:S(2)}) copy-start(bf16[4,512,512]{2,1,0:T(8,128)(2,1)} %refs_3_.1) | copy-start | bytes 6291460
  4.4 73.5 %copy-start.1 = (f32[4,512,512]{2,1,0:T(8,128)S(1)}, f32[4,512,512]{2,1,0:T(8,128)}, u32[]{:S(2)}) copy-start(f32[4,512,512]{2,1,0:T(8,128)} %refs_2_.1) | copy-start | bytes 12582916
  4.4 73.5 %copy-start.4 = (s32[4,64]{1,0:T(4,128)S(1)}, s32[4,64]{1,0:T(4,128)}, u32[]{:S(2)}) copy-start(s32[4,64]{1,0:T(4,128)} %refs_0_.3) | copy-start | bytes 3076
  4.4 73.5 %copy-start.5 = (s32[4,64]{1,0:T(4,128)S(1)}, s32[4,64]{1,0:T(4,128)}, u32[]{:S(2)}) copy-start(s32[4,64]{1,0:T(4,128)} %refs_1_.3) | copy-start | bytes 3076
  77.9 2.2 %copy-start.3 = (f32[4,512,512]{2,1,0:T(8,128)S(1)}, f32[4,512,512]{2,1,0:T(8,128)}, u32[]{:S(2)}) copy-start(f32[4,512,512]{2,1,0:T(8,128)} %refs_4_.1) | copy-start | bytes 12582916
